TPU v7x, 32 devices: a whole 2x2x4 slice. The times are simulated.
32 devices in a mesh: hx: 2 (over x), hy: 4 (over y, core), vz: 4 (over z).
Axes of the slice: x: 2, y: 2, z: 4, core: 2. Of those that a mesh axis runs over, the one named last changes fastest.
Arguments:
- prognostic: float32 [5, 80, 4, 4, 4, 256], P(None, 'vz', None, None, 'hy', 'hx'), may hold values from -6 to 6
- metric: float32 [4, 4, 4, 256], P(None, None, 'hy', 'hx'), may hold values from 0.5 to 2
- first_flux: float32 [5, 5], replicated, may hold values from -2.5 to 2.5
- second_flux: float32 [5, 5], replicated, may hold values from -2.5 to 2.5
- neighbour_face: int32 [4, 4, 256], P(None, 'hy', 'hx'), may hold values from 0 to 3
- orientation: int32 [4, 4, 256], P(None, 'hy', 'hx'), may hold values from 0 to 1
- coupling: float32 [4, 80, 4, 4, 4, 256], P(None, None, 'vz', None, 'hy', 'hx'), may hold values from 0.1 to 1
- damping: float32 [4, 4, 4, 256], P('vz', None, 'hy', 'hx'), may hold values from 0.005 to 0.05
Outputs:
- updated: float32 [5, 80, 4, 4, 4, 256], P(None, 'vz', None, None, 'hy', 'hx')
All inputs are finite; a program needn't handle non-finite values.
Results may differ from a plain program's by a relative error of at most 0.0003.
Values sent between devices are 32-bit elements; how exact they have to be, the bound alone decides.
No kernel may reach another device: no remote copies, remote signals or barrier semaphores. Data moves between devices by JAX's collectives and lax.ppermute only.
A program may use at most 64 MiB of HBM per device.

v0:
```python
import jax
import jax.numpy as jnp
import numpy as np
from jax import lax
from jax.sharding import PartitionSpec as P

step_size = 0.05
rusanov_speed = 1.0
lift_weight = 6.0
gravity_couple = 0.5
density_couple = 0.3
theta_couple = 0.4


def extended(x, sides, width):
    for axis, dim in sides:
        size, length = (lax.axis_size(axis), x.shape[dim])
        up = [(i, (i + 1) % size) for i in range(size)]
        down = [(j, i) for i, j in up]
        last = lax.slice_in_dim(x, length - width, length, axis=dim)
        initial = lax.slice_in_dim(x, 0, width, axis=dim)
        before = lax.ppermute(last, axis, up)
        after = lax.ppermute(initial, axis, down)
        x = jnp.concatenate([before, x, after], axis=dim)
    return x


def derivative_table():
    points = np.array([-1.0, -1.0 / np.sqrt(5.0), 1.0 / np.sqrt(5.0), 1.0])
    number = points.shape[0]
    barycentric = np.ones(number)
    for source in range(number):
        for another in range(number):
            if another != source:
                barycentric[source] = barycentric[source] / (points[source] - points[another])
    matrix = np.zeros((number, number))
    for target in range(number):
        for source in range(number):
            if target != source:
                matrix[target, source] = (
                    barycentric[source] / barycentric[target] / (points[target] - points[source])
                )
        matrix[target, target] = -np.sum(matrix[target])
    return jnp.asarray(matrix, dtype=jnp.float32)


def face_traces(fields):
    west_face = fields[:, :, :, 0]
    east_face = fields[:, :, :, -1]
    south_face = fields[:, :, 0, :]
    north_face = fields[:, :, -1, :]
    return jnp.stack([west_face, east_face, south_face, north_face], axis=2)


def pick_face(candidates, table_row, flip_row):
    chosen = jnp.zeros(candidates.shape[:2] + candidates.shape[3:], candidates.dtype)
    for option in range(candidates.shape[2]):
        chosen = chosen + jnp.where(table_row == option, candidates[:, :, option], 0.0)
    reverse = chosen[:, :, ::-1]
    return jnp.where(flip_row == 1, reverse, chosen)


def section_values(fields, outer_traces, metric, first_flux, second_flux):
    derivative = derivative_table()
    highest = lax.Precision.HIGHEST
    flux_first = jnp.einsum("fg,gljiab->fljiab", first_flux, fields, precision=highest)
    flux_second = jnp.einsum("fg,gljiab->fljiab", second_flux, fields, precision=highest)
    divergence = jnp.einsum("ci,fljiab->fljcab", derivative, flux_first, precision=highest)
    divergence = divergence + jnp.einsum(
        "cj,fljiab->flciab", derivative, flux_second, precision=highest
    )
    own_traces = face_traces(fields)
    own_first = face_traces(flux_first)
    own_second = face_traces(flux_second)
    own_normal = jnp.stack(
        [-own_first[:, :, 0], own_first[:, :, 1], -own_second[:, :, 2], own_second[:, :, 3]], axis=2
    )
    outer_first = jnp.einsum(
        "fg,glhkab->flhkab", first_flux, outer_traces[:, :, 0:2], precision=highest
    )
    outer_second = jnp.einsum(
        "fg,glhkab->flhkab", second_flux, outer_traces[:, :, 2:4], precision=highest
    )
    outer_normal = jnp.concatenate(
        [
            -outer_first[:, :, 0:1],
            outer_first[:, :, 1:2],
            -outer_second[:, :, 0:1],
            outer_second[:, :, 1:2],
        ],
        axis=2,
    )
    correction = 0.5 * (own_normal - outer_normal) + 0.5 * rusanov_speed * (
        outer_traces - own_traces
    )
    blank_face = jnp.zeros_like(correction[:, :, 0])
    middle_blanks = [blank_face] * (fields.shape[3] - 2)
    across_first = jnp.stack([correction[:, :, 0]] + middle_blanks + [correction[:, :, 1]], axis=3)
    across_second = jnp.stack([correction[:, :, 2]] + middle_blanks + [correction[:, :, 3]], axis=2)
    tendency = metric * (lift_weight * (across_first + across_second) - divergence)
    return fields + step_size * tendency


def level_difference(column_values):
    upper_part = jnp.concatenate([column_values[1:], jnp.zeros_like(column_values[:1])], axis=0)
    lower_part = jnp.concatenate([jnp.zeros_like(column_values[:1]), column_values[:-1]], axis=0)
    return upper_part - lower_part


def solve_unrolled(entry_a, entry_b, centre, entry_d, entry_e, source):
    levels = source.shape[0]
    empty_row = jnp.zeros_like(source[0])
    far_ratio, far_second, far_value = (empty_row, empty_row, empty_row)
    near_ratio, near_second, near_value = (empty_row, empty_row, empty_row)
    ratios, seconds, scaled = ([], [], [])
    for height in range(levels):
        reduced = entry_b[height] - entry_a[height] * far_ratio
        pivot_entry = centre[height] - entry_a[height] * far_second - reduced * near_ratio
        upper_ratio = (entry_d[height] - reduced * near_second) / pivot_entry
        second_ratio = entry_e[height] / pivot_entry
        scaled_value = (
            source[height] - entry_a[height] * far_value - reduced * near_value
        ) / pivot_entry
        far_ratio, far_second, far_value = (near_ratio, near_second, near_value)
        near_ratio, near_second, near_value = (upper_ratio, second_ratio, scaled_value)
        ratios.append(upper_ratio)
        seconds.append(second_ratio)
        scaled.append(scaled_value)
    next_one, next_two = (empty_row, empty_row)
    solution = [None] * levels
    for height in range(levels - 1, -1, -1):
        solved = scaled[height] - ratios[height] * next_one - seconds[height] * next_two
        solution[height] = solved
        next_two, next_one = (next_one, solved)
    return jnp.stack(solution)


def per_device(
    prognostic, metric, first_flux, second_flux, neighbour_face, orientation, coupling, damping
):
    own_traces = face_traces(prognostic)
    extent_first = own_traces.shape[4]
    extent_second = own_traces.shape[5]
    tables = jnp.stack([neighbour_face, orientation], axis=0)
    table_rims = extended(tables, (("hx", 3), ("hy", 2)), 1)
    inner_cols = slice(1, extent_second + 1)
    inner_rows = slice(1, extent_first + 1)
    for_west = pick_face(
        own_traces, table_rims[0, 1, 0:1, inner_cols], table_rims[1, 1, 0:1, inner_cols]
    )
    for_east = pick_face(
        own_traces,
        table_rims[0, 0, extent_first + 1 :, inner_cols],
        table_rims[1, 0, extent_first + 1 :, inner_cols],
    )
    chosen_first = extended(jnp.concatenate([for_west, for_east], axis=3), (("hy", 3),), 1)
    inner_west = pick_face(
        own_traces[..., : extent_first - 1, :], neighbour_face[0, 1:], orientation[0, 1:]
    )
    inner_east = pick_face(
        own_traces[..., 1:, :],
        neighbour_face[1, : extent_first - 1],
        orientation[1, : extent_first - 1],
    )
    west_outer = jnp.concatenate([chosen_first[:, :, :, 0:1], inner_west], axis=3)
    east_outer = jnp.concatenate([inner_east, chosen_first[:, :, :, 3:4]], axis=3)
    for_south = pick_face(
        own_traces[..., :, 0:1],
        table_rims[0, 3, inner_rows, 0:1],
        table_rims[1, 3, inner_rows, 0:1],
    )
    for_north = pick_face(
        own_traces[..., :, extent_second - 1 :],
        table_rims[0, 2, inner_rows, extent_second + 1 :],
        table_rims[1, 2, inner_rows, extent_second + 1 :],
    )
    chosen_second = extended(jnp.concatenate([for_south, for_north], axis=4), (("hx", 4),), 1)
    inner_south = pick_face(
        own_traces[..., :, : extent_second - 1], neighbour_face[2, :, 1:], orientation[2, :, 1:]
    )
    inner_north = pick_face(
        own_traces[..., :, 1:],
        neighbour_face[3, :, : extent_second - 1],
        orientation[3, :, : extent_second - 1],
    )
    south_outer = jnp.concatenate([chosen_second[..., 0:1], inner_south], axis=4)
    north_outer = jnp.concatenate([inner_north, chosen_second[..., 3:4]], axis=4)
    outer_traces = jnp.stack([west_outer, east_outer, south_outer, north_outer], axis=2)
    section_state = section_values(prognostic, outer_traces, metric, first_flux, second_flux)
    columns = lax.all_to_all(section_state[3:5], "vz", split_axis=2, concat_axis=1, tiled=True)
    source = columns[0] - gravity_couple * level_difference(columns[1])
    centre = coupling[0] + coupling[1] + coupling[2] + coupling[3] + damping[None]
    vertical_speed = solve_unrolled(
        -coupling[0], -coupling[1], centre, -coupling[2], -coupling[3], source
    )
    speed_jump = level_difference(vertical_speed)
    returned = lax.all_to_all(
        jnp.stack([vertical_speed, speed_jump]), "vz", split_axis=1, concat_axis=2, tiled=True
    )
    speed_here = returned[0]
    jump_here = returned[1]
    return jnp.stack(
        [
            section_state[0] - density_couple * jump_here,
            section_state[1],
            section_state[2],
            speed_here,
            section_state[4] - theta_couple * jump_here,
        ]
    )


def solution(mesh):
    placed = (
        P(None, "vz", None, None, "hy", "hx"),
        P(None, None, "hy", "hx"),
        P(),
        P(),
        P(None, "hy", "hx"),
        P(None, "hy", "hx"),
        P(None, None, "vz", None, "hy", "hx"),
        P("vz", None, "hy", "hx"),
    )
    return jax.shard_map(
        per_device,
        mesh=mesh,
        in_specs=placed,
        out_specs=P(None, "vz", None, None, "hy", "hx"),
        check_vma=False,
    )
```

profile of v0, /device:TPU:0, one launch (start us, length us, event | category | flops | bytes accessed | tf_op | source)
XLA Modules:
  0.0 132.3 jit_solution(14023152346951049371)
XLA Ops:
  0.0 0.9 pad_add_fusion.1
  0.9 2.9 %collective-permute-start.1 = (s32[2,4,1,1]{3,1,2,0:T(4,128)S(1)}, s32[2,4,1,1]{3,1,2,0:T(4,128)S(1)}, u32[]{:S(2)}, u32[]{:S(2)}) collective-permute-start(s32[2,4,1,1]{3,1,2,0:T(4,128)S(1)} %get-tuple-element.856), channel_id=1, source_target_pairs={{16,0},{0,16},{17,1},{1,17},{18,2},{2,18},{19,3},{3,19},{20,4},{4,... | collective-permute-start | bytes 104 | tf_op jit(solution)/shard_map/ppermute | solution.py:23
  3.9 1.3 fusion.1370
  5.2 1.1 fusion.1368
  6.5 1.1 fusion.1369
  8.0 1.7 %fusion.2 = f32[5,20,4,4,128]{4,0,3,2,1:T(8,128)S(1)} fusion(f32[5,20,4,4,128]{4,3,2,1,0:T(4,128)S(1)} %bitcast.7054, f32[5,5]{1,0:T(8,128)S(1)} %copy-done.31), kind=kOutput, calls=%fused_computation.2 | convolution fusion | flops 12288000 | bytes 1638500 | tf_op jit(solution)/shard_map/fg,gljiab->fljiab/dot_general | solution.py:66
  9.6 0.8 fusion.46
  10.4 0.8 slice_bitcast_fusion.6
  11.2 1.6 %fusion = f32[5,20,4,4,128]{4,0,3,2,1:T(8,128)S(1)} fusion(f32[5,20,4,4,128]{4,3,2,1,0:T(4,128)S(1)} %bitcast.7055, f32[5,5]{1,0:T(8,128)S(1)} %copy-done), kind=kOutput, calls=%fused_computation | convolution fusion | flops 12288000 | bytes 1638500 | tf_op jit(solution)/shard_map/fg,gljiab->fljiab/dot_general | solution.py:67
  13.0 0.9 slice_negate_fusion.2
  13.9 0.8 copy.1987
  14.7 0.8 copy.1988
  15.5 2.9 %fusion.12 = f32[5,20,4,128,4]{3,4,2,1,0:T(4,128)} fusion(f32[4,4,1,1,1]{1,0,4,3,2:T(4,128)S(1)} %copy-done.46, f32[5,20,4,4,128]{4,0,3,2,1:T(8,128)S(1)} %fusion), kind=kOutput, calls=%fused_computation.20 | convolution fusion | flops 9830400 | bytes 1638464 | tf_op jit(solution)/shard_map/cj,fljiab->flciab/dot_general | solution.py:69
  19.4 0.8 reverse_select_fusion.2
  29.2 0.9 collective-permute-start.2
  30.1 1.3 %fusion.44 = (f32[5,20,1,4,1,1]{5,0,3,1,4,2:T(8,128)}, f32[5,20,1,4,1,1]{5,0,3,1,4,2:T(8,128)}) fusion(f32[5,20,1,4,1,128]{5,0,3,1,4,2:T(8,128)S(1)} %get-tuple-element.871, f32[5,20,1,4,1,128]{5,0,3,1,4,2:T(8,128)S(1)} %get-tuple-element.872, f32[5,20,1,4,1,1]{5,4,3,2,1,0:T(1,128)S(1)} %get-tuple-element.738, ...), kind=kLoop, calls=%fused_computation.74 | loop fusion | flops 5600 | bytes 16008 | tf_op jit(solution)/shard_map/add | solution.py:58
  31.4 1.2 copy.1591
  32.6 1.1 copy.1592
  34.4 1.8 %reverse_select_fusion.3 = f32[5,20,4,1,1]{4,0,2,1,3:T(8,128)} fusion(f32[5,20,4,1,1]{4,0,2,1,3:T(8,128)} %copy.1592, pred[]{:T(512)} %bitcast.34), kind=kLoop, calls=%fused_computation.32 | loop fusion | flops 400 | bytes 3201 | tf_op jit(solution)/shard_map/jit(_where)/select_n | solution.py:60
  36.3 1.6 %collective-permute-start.6 = (f32[5,20,4,1,1]{4,0,2,1,3:T(8,128)}, f32[5,20,4,1,1]{4,0,2,1,3:T(8,128)}, u32[]{:S(2)}, u32[]{:S(2)}) collective-permute-start(f32[5,20,4,1,1]{4,0,2,1,3:T(8,128)} %reverse_select_fusion.3), channel_id=1, source_target_pairs={{0,16},{16,0},{1,17},{17,1},{2,18},{18,2},{3,19},{19,3},{4,20},{20... | collective-permute-start | bytes 4808 | tf_op jit(solution)/shard_map/ppermute | solution.py:22
  37.9 1.2 copy.1600
  39.1 1.1 copy.1601
  40.8 1.1 reverse_select_fusion
  42.4 4.5 %collective-permute-done.6 = f32[5,20,4,1,1]{4,0,2,1,3:T(8,128)} collective-permute-done((f32[5,20,4,1,1]{4,0,2,1,3:T(8,128)}, f32[5,20,4,1,1]{4,0,2,1,3:T(8,128)}, u32[]{:S(2)}, u32[]{:S(2)}) %collective-permute-start.6) | collective-permute-done | bytes 1632 | tf_op jit(solution)/shard_map/ppermute | solution.py:22
  46.9 1.2 maximum_bitcast_fusion.4
  48.2 5.7 %collective-permute-done.7 = f32[5,20,4,1,1]{4,0,2,1,3:T(8,128)S(1)} collective-permute-done((f32[5,20,4,1,1]{4,0,2,1,3:T(8,128)S(1)}, f32[5,20,4,1,1]{4,0,2,1,3:T(8,128)S(1)}, u32[]{:S(2)}, u32[]{:S(2)}) %collective-permute-start.7) | collective-permute-done | bytes 1632 | tf_op jit(solution)/shard_map/ppermute | solution.py:23
  54.7 0.8 compare_bitcast_fusion.19
  55.5 0.8 compare_bitcast_fusion.14
  56.9 1.7 %collective-permute-start.5 = (f32[5,20,4,1,128]{4,0,2,1,3:T(8,128)S(1)}, f32[5,20,4,1,128]{4,0,2,1,3:T(8,128)S(1)}, u32[]{:S(2)}, u32[]{:S(2)}) collective-permute-start(f32[5,20,4,1,128]{4,0,2,1,3:T(8,128)S(1)} %reverse_select_fusion.4), channel_id=1, source_target_pairs={{4,0},{8,4},{12,8},{0,12},{5,1},{9,5},{13,9},{1,13},{6,2},{10,6},{... | collective-permute-start | bytes 614408 | tf_op jit(solution)/shard_map/ppermute | solution.py:23
  58.6 6.2 %collective-permute-done.3 = f32[5,20,4,1,128]{4,0,2,1,3:T(8,128)S(1)} collective-permute-done((f32[5,20,4,1,128]{4,0,2,1,3:T(8,128)S(1)}, f32[5,20,4,1,128]{4,0,2,1,3:T(8,128)S(1)}, u32[]{:S(2)}, u32[]{:S(2)}) %collective-permute-start.3) | collective-permute-done | bytes 204832 | tf_op jit(solution)/shard_map/ppermute | solution.py:22
  64.9 0.8 collective-permute-done.5
  69.1 2.3 %fusion.10 = f32[5,20,4,4,1,128]{5,3,2,1,0,4:T(4,128)S(1)} fusion(f32[5,20,4,4,1,128]{5,3,2,1,0,4:T(4,128)S(1)} %bitcast.7056, f32[4,4,1,1,1]{1,0,4,3,2:T(4,128)S(1)} %copy-done.47, f32[5,20,4,1,1,128]{5,3,2,1,0,4:T(1,128)S(1)} %copy.1604, f32[5,20,4,1,1,128]{5,3,2,1,0,4:T(1,128)S(1)} %copy.1603, f32[5,20,1,4,1,128]{5,3,2,1,0,4:T(4,128)S(1)} %copy.1606, ...), kind=kOutput, calls=%fused_computation.16 | convolution fusion | flops 12083200 | bytes 4104272 | tf_op jit(solution)/shard_map/ci,fljiab->fljcab/dot_general | solution.py:68
  71.5 0.9 copy-done.24
  72.4 0.8 copy.1612
  73.2 4.9 %all-to-all-start = ((f32[2,20,4,4,1,128]{5,3,1,0,4,2:T(4,128)}), f32[2,20,4,4,1,128]{5,3,1,0,4,2:T(4,128)S(1)}, u32[]{:S(2)}, u32[]{:S(2)}) async-start(f32[2,20,4,4,1,128]{5,3,1,0,4,2:T(4,128)} %copy.1612), calls=%async_computation | async-start | bytes 655360 | tf_op jit(solution)/shard_map/all_to_all | solution.py:190
  78.8 10.8 %all-to-all-done = f32[2,20,4,4,1,128]{5,3,1,0,4,2:T(4,128)S(1)} async-done(((f32[2,20,4,4,1,128]{5,3,1,0,4,2:T(4,128)}), f32[2,20,4,4,1,128]{5,3,1,0,4,2:T(4,128)S(1)}, u32[]{:S(2)}, u32[]{:S(2)}) %all-to-all-start) | async-done | bytes 327712 | tf_op jit(solution)/shard_map/all_to_all | solution.py:190
  90.1 0.8 fusion.403
  90.9 0.8 fusion.396
  92.4 0.8 fusion.382
  93.1 0.8 fusion.375
  95.4 0.8 fusion.354
  97.6 0.8 fusion.333
  100.7 0.8 fusion.305
  102.2 1.0 bitcast_subtract_fusion.54
  116.2 13.0 %all_to_all.30 = f32[2,80,1,4,1,128]{5,3,4,2,0,1:T(4,128)S(1)} all-to-all(f32[2,80,1,4,1,128]{5,3,4,2,0,1:T(4,128)S(1)} %copy.1971), channel_id=1, replica_groups=mesh['hx'=2,'hy'=4,'vz'=4] {'vz'}, dimensions={1} | all-to-all | bytes 655360 | tf_op jit(solution)/shard_map/all_to_all | solution.py:197
  129.3 1.0 slice_subtract_fusion
  130.3 1.0 fusion.51
  131.3 1.1 pad_maximum_fusion
  (211 shorter events, 31.4 us)
Async XLA Ops:
  0.0 11.2 %copy-start = (f32[5,5]{1,0:T(8,128)S(1)}, f32[5,5]{1,0:T(8,128)}, u32[]{:S(2)}) copy-start(f32[5,5]{1,0:T(8,128)} %param.12) | copy-start | bytes 304
  0.0 6.4 %copy-start.34 = (s32[4,1,128]{2,1,0:T(1,128)S(1)}, s32[4,1,128]{2,1,0:T(1,128)}, u32[]{:S(2)}) copy-start(s32[4,1,128]{2,1,0:T(1,128)} %param.13) | copy-start | bytes 6148
  0.0 5.2 %copy-start.1 = (f32[5,20,4,4,1,128]{5,4,3,2,1,0:T(1,128)S(1)}, f32[5,20,4,4,1,128]{5,4,3,2,1,0:T(1,128)}, u32[]{:S(2)}) copy-start(f32[5,20,4,4,1,128]{5,4,3,2,1,0:T(1,128)} %param.9) | copy-start | bytes 2457604
  0.9 21.3 %collective-permute-start.1 = (s32[2,4,1,1]{3,1,2,0:T(4,128)S(1)}, s32[2,4,1,1]{3,1,2,0:T(4,128)S(1)}, u32[]{:S(2)}, u32[]{:S(2)}) collective-permute-start(s32[2,4,1,1]{3,1,2,0:T(4,128)S(1)} %get-tuple-element.856), channel_id=1, source_target_pairs={{16,0},{0,16},{17,1},{1,17},{18,2},{2,18},{19,3},{3,19},{20,4},{4,... | collective-permute-start | bytes 104 | tf_op jit(solution)/shard_map/ppermute | solution.py:23
  3.8 20.1 %collective-permute-start = (s32[2,4,1,1]{3,1,2,0:T(4,128)S(1)}, s32[2,4,1,1]{3,1,2,0:T(4,128)S(1)}, u32[]{:S(2)}, u32[]{:S(2)}) collective-permute-start(s32[2,4,1,1]{3,1,2,0:T(4,128)S(1)} %get-tuple-element.857), channel_id=1, source_target_pairs={{0,16},{16,0},{1,17},{17,1},{2,18},{18,2},{3,19},{19,3},{4,20},{20... | collective-permute-start | bytes 104 | tf_op jit(solution)/shard_map/ppermute | solution.py:22
  5.2 13.5 %copy-start.7 = (f32[5,20,4,1,1,128]{5,4,3,2,1,0:T(1,128)}, f32[5,20,4,1,1,128]{5,4,3,2,1,0:T(1,128)S(1)}, u32[]{:S(2)}) copy-start(f32[5,20,4,1,1,128]{5,4,3,2,1,0:T(1,128)S(1)} %get-tuple-element.745) | copy-start | bytes 614404
  5.2 13.5 %copy-start.9 = (f32[5,20,4,1,1,128]{5,4,3,2,1,0:T(1,128)}, f32[5,20,4,1,1,128]{5,4,3,2,1,0:T(1,128)S(1)}, u32[]{:S(2)}) copy-start(f32[5,20,4,1,1,128]{5,4,3,2,1,0:T(1,128)S(1)} %get-tuple-element.746) | copy-start | bytes 614404
  5.2 2.3 %copy-start.33 = (s32[4,1,128]{2,1,0:T(1,128)S(1)}, s32[4,1,128]{2,1,0:T(1,128)}, u32[]{:S(2)}) copy-start(s32[4,1,128]{2,1,0:T(1,128)} %param.14) | copy-start | bytes 6148
  6.4 1.6 %copy-start.31 = (f32[5,5]{1,0:T(8,128)S(1)}, f32[5,5]{1,0:T(8,128)}, u32[]{:S(2)}) copy-start(f32[5,5]{1,0:T(8,128)} %param.11) | copy-start | bytes 304
  13.0 2.5 %copy-start.46 = (f32[4,4,1,1,1]{1,0,4,3,2:T(4,128)S(1)}, f32[4,4,1,1,1]{1,0,4,3,2:T(4,128)}, u32[]{:S(2)}) copy-start(f32[4,4,1,1,1]{1,0,4,3,2:T(4,128)} %constant.65) | copy-start | bytes 196
  13.9 4.5 %copy-start.6 = (f32[4,80,1,4,1,128]{5,4,3,2,1,0:T(1,128)S(1)}, f32[4,80,1,4,1,128]{5,4,3,2,1,0:T(1,128)}, u32[]{:S(2)}) copy-start(f32[4,80,1,4,1,128]{5,4,3,2,1,0:T(1,128)} %param.15) | copy-start | bytes 1966084
  15.5 3.1 %copy-start.45 = (f32[1,4,1,128]{3,2,1,0:T(1,128)S(1)}, f32[1,4,1,128]{3,2,1,0:T(1,128)}, u32[]{:S(2)}) copy-start(f32[1,4,1,128]{3,2,1,0:T(1,128)} %param.16) | copy-start | bytes 6148
  18.5 3.0 %copy-start.11 = (f32[1,80,1,4,1,128]{5,3,4,2,1,0:T(4,128)}, f32[1,80,1,4,1,128]{5,3,4,2,1,0:T(4,128)S(1)}, u32[]{:S(2)}) copy-start(f32[1,80,1,4,1,128]{5,3,4,2,1,0:T(4,128)S(1)} %get-tuple-element.749) | copy-start | bytes 491524
  18.5 3.0 %copy-start.13 = (f32[1,80,1,4,1,128]{5,3,4,2,1,0:T(4,128)}, f32[1,80,1,4,1,128]{5,3,4,2,1,0:T(4,128)S(1)}, u32[]{:S(2)}) copy-start(f32[1,80,1,4,1,128]{5,3,4,2,1,0:T(4,128)S(1)} %get-tuple-element.747) | copy-start | bytes 491524
  18.6 71.5 %copy-start.2 = (f32[1,80,1,4,1,128]{5,3,4,2,1,0:T(4,128)}, f32[1,80,1,4,1,128]{5,3,4,2,1,0:T(4,128)S(1)}, u32[]{:S(2)}) copy-start(f32[1,80,1,4,1,128]{5,3,4,2,1,0:T(4,128)S(1)} %get-tuple-element.750) | copy-start | bytes 491524
  18.6 71.5 %copy-start.4 = (f32[1,80,1,4,1,128]{5,3,4,2,1,0:T(4,128)}, f32[1,80,1,4,1,128]{5,3,4,2,1,0:T(4,128)S(1)}, u32[]{:S(2)}) copy-start(f32[1,80,1,4,1,128]{5,3,4,2,1,0:T(4,128)S(1)} %get-tuple-element.748) | copy-start | bytes 491524
  18.7 2.9 %copy-start.15 = (f32[80,1,4,1,128]{4,2,3,1,0:T(4,128)}, f32[80,1,4,1,128]{4,2,3,1,0:T(4,128)S(1)}, u32[]{:S(2)}) copy-start(f32[80,1,4,1,128]{4,2,3,1,0:T(4,128)S(1)} %bitcast_add_fusion) | copy-start | bytes 491524
  29.2 25.5 %collective-permute-start.2 = (s32[2,4,1,130]{3,1,2,0:T(4,128)}, s32[2,4,1,130]{3,1,2,0:T(4,128)}, u32[]{:S(2)}, u32[]{:S(2)}) collective-permute-start(s32[2,4,1,130]{3,1,2,0:T(4,128)} %pad_add_fusion), channel_id=1, source_target_pairs={{4,0},{8,4},{12,8},{0,12},{5,1},{9,5},{13,9},{1,13},{6,2},{10,6},{... | collective-permute-start | bytes 12488 | tf_op jit(solution)/shard_map/ppermute | solution.py:23
  30.1 25.4 %collective-permute-start.4 = (s32[2,4,1,130]{3,1,2,0:T(4,128)}, s32[2,4,1,130]{3,1,2,0:T(4,128)}, u32[]{:S(2)}, u32[]{:S(2)}) collective-permute-start(s32[2,4,1,130]{3,1,2,0:T(4,128)} %pad_add_fusion), channel_id=1, source_target_pairs={{0,4},{4,8},{8,12},{12,0},{1,5},{5,9},{9,13},{13,1},{2,6},{6,10},{... | collective-permute-start | bytes 12488 | tf_op jit(solution)/shard_map/ppermute | solution.py:22
  36.3 10.6 %collective-permute-start.6 = (f32[5,20,4,1,1]{4,0,2,1,3:T(8,128)}, f32[5,20,4,1,1]{4,0,2,1,3:T(8,128)}, u32[]{:S(2)}, u32[]{:S(2)}) collective-permute-start(f32[5,20,4,1,1]{4,0,2,1,3:T(8,128)} %reverse_select_fusion.3), channel_id=1, source_target_pairs={{0,16},{16,0},{1,17},{17,1},{2,18},{18,2},{3,19},{19,3},{4,20},{20... | collective-permute-start | bytes 4808 | tf_op jit(solution)/shard_map/ppermute | solution.py:22
  40.2 13.6 %copy-start.23 = (f32[5,20,4,1,127]{4,0,2,1,3:T(8,128)S(1)}, f32[5,20,4,1,127]{4,0,2,1,3:T(8,128)}, u32[]{:S(2)}) copy-start(f32[5,20,4,1,127]{4,0,2,1,3:T(8,128)} %reverse_select_fusion.1) | copy-start | bytes 609604
  42.0 11.9 %collective-permute-start.7 = (f32[5,20,4,1,1]{4,0,2,1,3:T(8,128)S(1)}, f32[5,20,4,1,1]{4,0,2,1,3:T(8,128)S(1)}, u32[]{:S(2)}, u32[]{:S(2)}) collective-permute-start(f32[5,20,4,1,1]{4,0,2,1,3:T(8,128)S(1)} %reverse_select_fusion), channel_id=1, source_target_pairs={{16,0},{0,16},{17,1},{1,17},{18,2},{2,18},{19,3},{3,19},{20,4},{4,... | collective-permute-start | bytes 4808 | tf_op jit(solution)/shard_map/ppermute | solution.py:23
  48.1 8.1 %copy-start.8 = (f32[5,20,4,1,1,128]{5,4,3,2,1,0:T(1,128)S(1)}, f32[5,20,4,1,1,128]{5,4,3,2,1,0:T(1,128)}, u32[]{:S(2)}) copy-start(f32[5,20,4,1,1,128]{5,4,3,2,1,0:T(1,128)} %copy-done.7) | copy-start | bytes 614404
  48.1 8.1 %copy-start.10 = (f32[5,20,4,1,1,128]{5,4,3,2,1,0:T(1,128)S(1)}, f32[5,20,4,1,1,128]{5,4,3,2,1,0:T(1,128)}, u32[]{:S(2)}) copy-start(f32[5,20,4,1,1,128]{5,4,3,2,1,0:T(1,128)} %copy-done.9) | copy-start | bytes 614404
  56.6 9.1 %copy-start.32 = (f32[5,5]{1,0:T(8,128)S(1)}, f32[5,5]{1,0:T(8,128)}, u32[]{:S(2)}) copy-start(f32[5,5]{1,0:T(8,128)} %param.11) | copy-start | bytes 304
  56.7 8.2 %collective-permute-start.3 = (f32[5,20,4,1,128]{4,0,2,1,3:T(8,128)S(1)}, f32[5,20,4,1,128]{4,0,2,1,3:T(8,128)S(1)}, u32[]{:S(2)}, u32[]{:S(2)}) collective-permute-start(f32[5,20,4,1,128]{4,0,2,1,3:T(8,128)S(1)} %reverse_select_fusion.5), channel_id=1, source_target_pairs={{0,4},{4,8},{8,12},{12,0},{1,5},{5,9},{9,13},{13,1},{2,6},{6,10},{... | collective-permute-start | bytes 614408 | tf_op jit(solution)/shard_map/ppermute | solution.py:22
  56.9 8.8 %collective-permute-start.5 = (f32[5,20,4,1,128]{4,0,2,1,3:T(8,128)S(1)}, f32[5,20,4,1,128]{4,0,2,1,3:T(8,128)S(1)}, u32[]{:S(2)}, u32[]{:S(2)}) collective-permute-start(f32[5,20,4,1,128]{4,0,2,1,3:T(8,128)S(1)} %reverse_select_fusion.4), channel_id=1, source_target_pairs={{4,0},{8,4},{12,8},{0,12},{5,1},{9,5},{13,9},{1,13},{6,2},{10,6},{... | collective-permute-start | bytes 614408 | tf_op jit(solution)/shard_map/ppermute | solution.py:23
  72.4 5.7 %copy-start.12 = (f32[1,80,1,4,1,128]{5,3,4,2,1,0:T(4,128)S(1)}, f32[1,80,1,4,1,128]{5,3,4,2,1,0:T(4,128)}, u32[]{:S(2)}) copy-start(f32[1,80,1,4,1,128]{5,3,4,2,1,0:T(4,128)} %copy-done.11) | copy-start | bytes 491524
  72.4 5.7 %copy-start.14 = (f32[1,80,1,4,1,128]{5,3,4,2,1,0:T(4,128)S(1)}, f32[1,80,1,4,1,128]{5,3,4,2,1,0:T(4,128)}, u32[]{:S(2)}) copy-start(f32[1,80,1,4,1,128]{5,3,4,2,1,0:T(4,128)} %copy-done.13) | copy-start | bytes 491524
  72.4 5.7 %copy-start.16 = (f32[80,1,4,1,128]{4,2,3,1,0:T(4,128)S(1)}, f32[80,1,4,1,128]{4,2,3,1,0:T(4,128)}, u32[]{:S(2)}) copy-start(f32[80,1,4,1,128]{4,2,3,1,0:T(4,128)} %copy-done.15) | copy-start | bytes 491524
  73.2 16.4 %all-to-all-start = ((f32[2,20,4,4,1,128]{5,3,1,0,4,2:T(4,128)}), f32[2,20,4,4,1,128]{5,3,1,0,4,2:T(4,128)S(1)}, u32[]{:S(2)}, u32[]{:S(2)}) async-start(f32[2,20,4,4,1,128]{5,3,1,0,4,2:T(4,128)} %copy.1612), calls=%async_computation | async-start | bytes 655360 | tf_op jit(solution)/shard_map/all_to_all | solution.py:190
  90.1 13.2 %copy-start.3 = (f32[1,80,1,4,1,128]{5,3,4,2,1,0:T(4,128)S(1)}, f32[1,80,1,4,1,128]{5,3,4,2,1,0:T(4,128)}, u32[]{:S(2)}) copy-start(f32[1,80,1,4,1,128]{5,3,4,2,1,0:T(4,128)} %copy-done.2) | copy-start | bytes 491524
  90.1 13.2 %copy-start.5 = (f32[1,80,1,4,1,128]{5,3,4,2,1,0:T(4,128)S(1)}, f32[1,80,1,4,1,128]{5,3,4,2,1,0:T(4,128)}, u32[]{:S(2)}) copy-start(f32[1,80,1,4,1,128]{5,3,4,2,1,0:T(4,128)} %copy-done.4) | copy-start | bytes 491524
  99.9 8.9 %copy-start.26 = (f32[4,128]{1,0:T(4,128)S(1)}, f32[4,128]{1,0:T(4,128)}, u32[]{:S(2)}) copy-start(f32[4,128]{1,0:T(4,128)} %get-tuple-element.713) | copy-start | bytes 6148
  99.9 8.9 %copy-start.27 = (f32[4,128]{1,0:T(4,128)S(1)}, f32[4,128]{1,0:T(4,128)}, u32[]{:S(2)}) copy-start(f32[4,128]{1,0:T(4,128)} %get-tuple-element.715) | copy-start | bytes 6148
  99.9 8.9 %copy-start.28 = (f32[4,128]{1,0:T(4,128)S(1)}, f32[4,128]{1,0:T(4,128)}, u32[]{:S(2)}) copy-start(f32[4,128]{1,0:T(4,128)} %get-tuple-element.719) | copy-start | bytes 6148
  99.9 8.9 %copy-start.29 = (f32[4,128]{1,0:T(4,128)S(1)}, f32[4,128]{1,0:T(4,128)}, u32[]{:S(2)}) copy-start(f32[4,128]{1,0:T(4,128)} %get-tuple-element.721) | copy-start | bytes 6148
  99.9 8.9 %copy-start.30 = (f32[4,128]{1,0:T(4,128)S(1)}, f32[4,128]{1,0:T(4,128)}, u32[]{:S(2)}) copy-start(f32[4,128]{1,0:T(4,128)} %get-tuple-element.724) | copy-start | bytes 6148
  99.9 8.9 %copy-start.40 = (f32[4,128]{1,0:T(4,128)S(1)}, f32[4,128]{1,0:T(4,128)}, u32[]{:S(2)}) copy-start(f32[4,128]{1,0:T(4,128)} %get-tuple-element.710) | copy-start | bytes 6148
  99.9 8.9 %copy-start.41 = (f32[4,128]{1,0:T(4,128)S(1)}, f32[4,128]{1,0:T(4,128)}, u32[]{:S(2)}) copy-start(f32[4,128]{1,0:T(4,128)} %get-tuple-element.711) | copy-start | bytes 6148
  100.0 8.9 %copy-start.42 = (f32[4,128]{1,0:T(4,128)S(1)}, f32[4,128]{1,0:T(4,128)}, u32[]{:S(2)}) copy-start(f32[4,128]{1,0:T(4,128)} %get-tuple-element.716) | copy-start | bytes 6148
  100.0 8.9 %copy-start.43 = (f32[4,128]{1,0:T(4,128)S(1)}, f32[4,128]{1,0:T(4,128)}, u32[]{:S(2)}) copy-start(f32[4,128]{1,0:T(4,128)} %get-tuple-element.717) | copy-start | bytes 6148
  100.0 8.9 %copy-start.44 = (f32[4,128]{1,0:T(4,128)S(1)}, f32[4,128]{1,0:T(4,128)}, u32[]{:S(2)}) copy-start(f32[4,128]{1,0:T(4,128)} %get-tuple-element.722) | copy-start | bytes 6148
  105.3 9.3 %copy-start.35 = (f32[4,128]{1,0:T(4,128)S(1)}, f32[4,128]{1,0:T(4,128)}, u32[]{:S(2)}) copy-start(f32[4,128]{1,0:T(4,128)} %get-tuple-element.712) | copy-start | bytes 6148
  105.3 9.3 %copy-start.36 = (f32[4,128]{1,0:T(4,128)S(1)}, f32[4,128]{1,0:T(4,128)}, u32[]{:S(2)}) copy-start(f32[4,128]{1,0:T(4,128)} %get-tuple-element.714) | copy-start | bytes 6148
  105.3 9.3 %copy-start.37 = (f32[4,128]{1,0:T(4,128)S(1)}, f32[4,128]{1,0:T(4,128)}, u32[]{:S(2)}) copy-start(f32[4,128]{1,0:T(4,128)} %get-tuple-element.718) | copy-start | bytes 6148
  105.3 9.3 %copy-start.38 = (f32[4,128]{1,0:T(4,128)S(1)}, f32[4,128]{1,0:T(4,128)}, u32[]{:S(2)}) copy-start(f32[4,128]{1,0:T(4,128)} %get-tuple-element.720) | copy-start | bytes 6148
  105.3 9.3 %copy-start.39 = (f32[4,128]{1,0:T(4,128)S(1)}, f32[4,128]{1,0:T(4,128)}, u32[]{:S(2)}) copy-start(f32[4,128]{1,0:T(4,128)} %get-tuple-element.723) | copy-start | bytes 6148
  (11 other events, 12.7 us)
where the time goes:
time: 134 us; the launch traced here: 132 us
  other arithmetic  42.9 us (32%)
  waiting for transfers between devices  28 us (21%)
  local copies, waits for them, and re-layouts  18.3 us (14%)
  blocking collectives  13 us (10%)
  starting transfers between devices  12.7 us (9%)
  matrix products  9.9 us (7%)
  between operations  7.52 us (6%)
    all_to_all x1, blocking collectives, per_device(): lax.all_to_all(jnp.stack([vertical_speed, speed_jump]), 'vz', split_axis=...  13 us
    div x21, other arithmetic, solve_unrolled(): (source[height] - entry_a[height] * far_value - reduced * near_value) / p...  12.6 us
    all_to_all x1, waiting for transfers between devices, per_device(): lax.all_to_all(section_state[3:5], 'vz', split_axis=2, concat_axis=1, til...  10.8 us
    ppermute x4, waiting for transfers between devices, extended(): before = lax.ppermute(last, axis, up)  10.7 us
    sub x34, other arithmetic, solve_unrolled(): scaled[height] - ratios[height] * next_one - seconds[height] * next_two  10.4 us
    ppermute x4, waiting for transfers between devices, extended(): after = lax.ppermute(initial, axis, down)  6.51 us
    ppermute x4, starting transfers between devices, extended(): after = lax.ppermute(initial, axis, down)  6 us
    all_to_all x1, starting transfers between devices, per_device(): lax.all_to_all(section_state[3:5], 'vz', split_axis=2, concat_axis=1, til...  4.87 us
  transfers between devices with their start and end apart: 9, of which 5 were waited for; matrix products, arithmetic and copies ran while one was open for 24% of the time, Pallas kernels for 0%

commit v1 on v0

v1 whole, which is shorter than its diff:
```python
import functools

import jax
import jax.numpy as jnp
import numpy as np
from jax import lax
from jax.experimental import pallas as pl
from jax.experimental.pallas import tpu as pltpu
from jax.sharding import PartitionSpec as P

step_size = 0.05
lift_weight = 6.0
gravity_couple = 0.5
density_couple = 0.3
theta_couple = 0.4

NODES = 4
POINTS = NODES * NODES
FIELDS = 5
FACE_POINTS = ((0, 4, 8, 12), (3, 7, 11, 15), (0, 1, 2, 3), (12, 13, 14, 15))
RIM_POINTS = tuple(sorted(set(sum(FACE_POINTS, ()))))
ROWS = 8


def derivative_table():
    points = np.array([-1.0, -1.0 / np.sqrt(5.0), 1.0 / np.sqrt(5.0), 1.0])
    number = points.shape[0]
    barycentric = np.ones(number)
    for source in range(number):
        for another in range(number):
            if another != source:
                barycentric[source] = barycentric[source] / (points[source] - points[another])
    matrix = np.zeros((number, number))
    for target in range(number):
        for source in range(number):
            if target != source:
                matrix[target, source] = (
                    barycentric[source] / barycentric[target] / (points[target] - points[source])
                )
        matrix[target, target] = -np.sum(matrix[target])
    return matrix


def operator_tables(lanes):
    weight = 0.5 * lift_weight
    table = derivative_table()
    table[0, 0] += weight
    table[-1, -1] -= weight
    eye = np.eye(NODES)
    along_first = np.kron(eye, table)
    along_second = np.kron(table, eye)
    ends = np.zeros(NODES)
    ends[0] = ends[-1] = 1.0
    faces = np.diag(np.kron(np.ones(NODES), ends) + np.kron(ends, np.ones(NODES)))
    first = np.zeros((POINTS, lanes))
    second = np.zeros((POINTS, lanes))
    same = np.zeros((FIELDS, POINTS, lanes))
    owner = np.full((lanes,), -1)
    for g in range(FIELDS):
        own = slice(POINTS * g, POINTS * (g + 1))
        first[:, own] = -along_first
        second[:, own] = -along_second
        same[g, :, own] = -weight * faces
        owner[own] = g
        for k in range(NODES):
            south = FIELDS * POINTS + 2 * NODES * g + k
            north = south + NODES
            second[FACE_POINTS[2][k], south] = weight
            second[FACE_POINTS[3][k], north] = -weight
            same[g, FACE_POINTS[2][k], south] = weight
            same[g, FACE_POINTS[3][k], north] = weight
            owner[south] = owner[north] = g
    tables = np.concatenate([first, second, same.reshape(FIELDS * POINTS, lanes)])
    return tables.astype(np.float32), owner


def chunks(total):
    return [min(start, total - ROWS) for start in range(0, total, ROWS)]


def pick(values, masks, flip):
    chosen = []
    for k in range(NODES):
        row = values[FACE_POINTS[0][k]]
        for option in range(1, 4):
            row = jnp.where(masks[option], values[FACE_POINTS[option][k]], row)
        chosen.append(row)
    return [jnp.where(flip, chosen[NODES - 1 - k], chosen[k]) for k in range(NODES)]


def table_masks(face_row, flip_row, lanes):
    face = jnp.broadcast_to(face_row, (ROWS, lanes))
    flip = jnp.broadcast_to(flip_row, (ROWS, lanes))
    return [face == option for option in range(4)], flip == 1


def edge_kernel(state, to_up, to_down):
    count, lanes = to_up.shape
    lane = lax.broadcasted_iota(jnp.int32, (ROWS, lanes), 1)
    for q in chunks(count):
        last = jnp.zeros((ROWS, lanes), jnp.float32)
        initial = last
        for point in RIM_POINTS:
            plane = state[pl.ds(q * POINTS + point, ROWS, stride=POINTS), :]
            moved = pltpu.roll(plane, point + 1, 1)
            last = jnp.where(lane == point, moved, last)
            initial = jnp.where(lane == point + 1, moved, initial)
        to_up[pl.ds(q, ROWS), :] = last
        to_down[pl.ds(q, ROWS), :] = initial


def face_kernel(state, table_west, table_east, to_west, to_east):
    count, lanes = state.shape
    sides = []
    for table, out in ((table_west, to_west), (table_east, to_east)):
        masks, flip = table_masks(table[0:1, :], table[1:2, :], lanes)
        sides.append((masks, flip, out))
    for q in chunks(count // POINTS):
        values = {
            point: state[pl.ds(q * POINTS + point, ROWS, stride=POINTS), :] for point in RIM_POINTS
        }
        for masks, flip, out in sides:
            for k, row in enumerate(pick(values, masks, flip)):
                out[pl.ds(q * NODES + k, ROWS, stride=NODES), :] = row


def element_kernel(
    state,
    from_down,
    from_up,
    neighbour_face,
    orientation,
    metric,
    first_flux,
    second_flux,
    tables,
    part,
    outer,
    operator_high,
    operator_low,
):
    levels = state.shape[0] // (FIELDS * POINTS)
    lanes = state.shape[1]
    lane = lax.broadcasted_iota(jnp.int32, (ROWS, lanes), 1)
    for side, (face, received, edge) in enumerate(((2, from_down, 0), (3, from_up, lanes - 1))):
        shift = 1 if side == 0 else lanes - 1
        row = neighbour_face[face : face + 1, :]
        way = orientation[face : face + 1, :]
        here, here_flip = table_masks(row, way, lanes)
        face_rows = jnp.broadcast_to(row, (ROWS, lanes))
        way_rows = jnp.broadcast_to(way, (ROWS, lanes))
        moved_face = pltpu.roll(face_rows, lanes - shift, 1)
        moved_way = pltpu.roll(way_rows, lanes - shift, 1)
        there = [moved_face == option for option in range(4)]
        there_flip = moved_way == 1
        for f in range(FIELDS):
            for start in chunks(levels):
                q = f * levels + start
                values = {
                    point: state[pl.ds(q * POINTS + point, ROWS, stride=POINTS), :]
                    for point in RIM_POINTS
                }
                packed = received[pl.ds(q, ROWS), :]
                beyond = {}
                for point in RIM_POINTS:
                    source = point if side == 0 else point + 1
                    beyond[point] = pltpu.roll(packed, (edge - source) % lanes, 1)
                inner = pick(values, there, there_flip)
                rim = pick(beyond, here, here_flip)
                for k in range(NODES):
                    row_k = jnp.where(lane == edge, rim[k], pltpu.roll(inner[k], shift, 1))
                    at = start * 8 * FIELDS + 8 * f + NODES * side + k
                    outer[pl.ds(at, ROWS, stride=8 * FIELDS), :] = row_k
    column = lax.broadcasted_iota(jnp.int32, (1, lanes), 1)
    own_columns = FIELDS * POINTS
    owner = jnp.where(column < own_columns, column // POINTS, (column - own_columns) // 8)
    for f in range(FIELDS):
        first_row = jnp.zeros((1, lanes), jnp.float32)
        second_row = first_row
        for g in range(FIELDS):
            first_row = jnp.where(owner == g, first_flux[f, g], first_row)
            second_row = jnp.where(owner == g, second_flux[f, g], second_row)
        block = (
            first_row * tables[0:POINTS, :]
            + second_row * tables[POINTS : 2 * POINTS, :]
            + tables[(2 + f) * POINTS : (3 + f) * POINTS, :]
        )
        high = block.astype(jnp.bfloat16)
        operator_high[f * POINTS : (f + 1) * POINTS, :] = high
        operator_low[f * POINTS : (f + 1) * POINTS, :] = (
            block - high.astype(jnp.float32)
        ).astype(jnp.bfloat16)
    high = operator_high[...]
    low = operator_low[...]
    scale = step_size * metric[...]
    blank = jnp.zeros((lanes - own_columns - 8 * FIELDS, lanes), jnp.float32)
    for pair in range(0, levels, 2):
        sides = []
        for level in (pair, pair + 1):
            rows = [
                state[pl.ds((f * levels + level) * POINTS, POINTS), :] for f in range(FIELDS)
            ]
            rows.append(outer[pl.ds(level * 8 * FIELDS, 8 * FIELDS), :])
            rows.append(blank)
            sides.append(jnp.concatenate(rows, axis=0))
        values = jnp.concatenate(sides, axis=1)
        top = values.astype(jnp.bfloat16)
        rest = (values - top.astype(jnp.float32)).astype(jnp.bfloat16)
        change = (
            jnp.dot(high, top, preferred_element_type=jnp.float32)
            + jnp.dot(high, rest, preferred_element_type=jnp.float32)
            + jnp.dot(low, top, preferred_element_type=jnp.float32)
        )
        for place, level in enumerate((pair, pair + 1)):
            for f in range(FIELDS):
                at = pl.ds((f * levels + level) * POINTS, POINTS)
                part[at, :] = (
                    state[at, :]
                    + scale
                    * change[
                        f * POINTS : (f + 1) * POINTS, place * lanes : (place + 1) * lanes
                    ]
                )


def first_side(part, from_west, from_east, flux, scale, f, start, j, i, levels):
    point = NODES * j + i
    value = part[pl.ds((f * levels + start) * POINTS + point, ROWS, stride=POINTS), :]
    if i in (0, NODES - 1):
        outer = from_west if i == 0 else from_east
        sign = 1.0 if i == 0 else -1.0
        total = None
        for g in range(FIELDS):
            rows = outer[pl.ds((g * levels + start) * NODES + j, ROWS, stride=NODES), :]
            factor = sign * flux[f, g] + (1.0 if f == g else 0.0)
            term = factor * rows
            total = term if total is None else total + term
        value = value + scale[point : point + 1, :] * total
    return value


def pack_kernel(
    nodes, part, from_west, from_east, metric, flux, theta, *rest
):
    ways = NODES
    sends, (blocks, column) = rest[:ways], rest[ways:]
    levels = part.shape[0] // (FIELDS * POINTS)
    lanes = part.shape[1]
    count = len(nodes)
    me = lax.axis_index("vz")
    scale = (0.5 * lift_weight * step_size) * metric[...]
    column[...] = jnp.zeros_like(column)
    for j in range(NODES):
        for place, i in enumerate(nodes):
            slot = j * count + place
            vertical = []
            for start in chunks(levels):
                args = (start, j, i, levels)
                vertical.append(first_side(part, from_west, from_east, flux, scale, 3, *args))
                heat = first_side(part, from_west, from_east, flux, scale, 4, *args)
                column[slot, pl.ds(ROWS + start, ROWS), :] = heat
                theta[pl.ds(start * POINTS + NODES * j + i, ROWS, stride=POINTS), :] = heat
            for start, speed in zip(chunks(levels), vertical):
                upper = column[slot, pl.ds(ROWS + start + 1, ROWS), :]
                lower = column[slot, pl.ds(ROWS + start - 1, ROWS), :]
                blocks[j, pl.ds(start * count + place, ROWS, stride=count), :] = (
                    speed - gravity_couple * (upper - lower)
                )
            for extra, level in ((0, 0), (1, levels - 1)):
                at = (levels + extra) * count + place
                blocks[j, at : at + 1, :] = column[slot, ROWS + level : ROWS + level + 1, :]
    for way in range(ways):
        sends[way][...] = blocks[me ^ way]


def finish_section_kernel(part, from_west, from_east, metric, flux, done):
    levels = part.shape[0] // (FIELDS * POINTS)
    scale = (0.5 * lift_weight * step_size) * metric[...]
    rows = 3 * levels * POINTS
    done[...] = part[0:rows, :]
    for f in range(3):
        for j in range(NODES):
            for i in (0, NODES - 1):
                for start in chunks(levels):
                    value = first_side(
                        part, from_west, from_east, flux, scale, f, start, j, i, levels
                    )
                    at = (f * levels + start) * POINTS + NODES * j + i
                    done[pl.ds(at, ROWS, stride=POINTS), :] = value


def factor_kernel(coupling, damping, far, near, inverse, ratio, second):
    levels = coupling.shape[1]
    shape = coupling.shape[2:]
    blank = jnp.zeros(shape, jnp.float32)
    far_ratio, far_second, near_ratio, near_second = (blank,) * 4
    extra = damping[...]
    for level in range(levels):
        a, b, d, e = (coupling[entry, level] for entry in range(4))
        centre = a + b + d + e + extra
        reduced = -b + a * far_ratio
        pivot = centre + a * far_second - reduced * near_ratio
        scaled = 1.0 / pivot
        upper_ratio = (-d - reduced * near_second) * scaled
        second_ratio = -e * scaled
        far[level] = a * scaled
        near[level] = reduced * scaled
        inverse[level] = scaled
        ratio[level] = upper_ratio
        second[level] = second_ratio
        far_ratio, far_second = near_ratio, near_second
        near_ratio, near_second = upper_ratio, second_ratio


def solve_kernel(far, near, inverse, ratio, second, *rest):
    ways = NODES
    received, sends, (source, heat, speed) = rest[:ways], rest[ways : 2 * ways], rest[2 * ways :]
    levels = far.shape[0]
    here = levels // ways
    me = lax.axis_index("vz")
    for way in range(ways):
        block = me ^ way
        source[pl.ds(block * here, here)] = received[way][0:here]
        heat[block] = received[way][here : here + 2]
    for block in range(ways - 1):
        last = block * here + here - 1
        source[last] = source[last] - gravity_couple * heat[block + 1, 0]
        source[last + 1] = source[last + 1] + gravity_couple * heat[block, 1]
    blank = jnp.zeros(far.shape[1:], jnp.float32)
    before_two, before_one = blank, blank
    for level in range(levels):
        value = source[level] * inverse[level]
        value = value + far[level] * before_two
        value = value - near[level] * before_one
        source[level] = value
        before_two, before_one = before_one, value
    speed[0] = blank
    speed[levels + 1] = blank
    next_one, next_two = blank, blank
    for level in range(levels - 1, -1, -1):
        value = source[level] - second[level] * next_two
        value = value - ratio[level] * next_one
        speed[level + 1] = value
        next_two, next_one = next_one, value
    for way in range(ways):
        sends[way][...] = speed[pl.ds((me ^ way) * here, here + 2)]


def update_kernel(nodes, done, theta, *rest):
    ways = NODES
    received, (out, speed) = rest[:ways], rest[ways:]
    levels = theta.shape[0] // POINTS
    size = levels * POINTS
    count = len(nodes)
    me = lax.axis_index("vz")
    for way in range(ways):
        speed[me ^ way] = received[way][...]
    out[size : 3 * size, :] = done[size : 3 * size, :]
    for j in range(NODES):
        for place, i in enumerate(nodes):
            point = NODES * j + i
            for start in chunks(levels):
                lower, value, upper = (
                    speed[j, pl.ds((start + k) * count + place, ROWS, stride=count), :]
                    for k in range(3)
                )
                jump = upper - lower
                at = pl.ds(start * POINTS + point, ROWS, stride=POINTS)
                out[pl.ds(start * POINTS + point, ROWS, stride=POINTS), :] = (
                    done[at, :] - density_couple * jump
                )
                out[pl.ds(3 * size + start * POINTS + point, ROWS, stride=POINTS), :] = value
                out[pl.ds(4 * size + start * POINTS + point, ROWS, stride=POINTS), :] = (
                    theta[at, :] - theta_couple * jump
                )


VMEM = pl.BlockSpec(memory_space=pltpu.VMEM)
SMEM = pl.BlockSpec(memory_space=pltpu.SMEM)


def call(kernel, outs, in_specs, scratch=(), cost=0, name=None):
    kinds = [pltpu.VMEM(shape, jnp.float32) for shape in outs]
    return pl.pallas_call(
        kernel,
        out_shape=kinds,
        in_specs=in_specs,
        out_specs=[VMEM] * len(outs),
        scratch_shapes=list(scratch),
        compiler_params=pltpu.CompilerParams(vmem_limit_bytes=24 * 1024 * 1024),
        cost_estimate=pl.CostEstimate(flops=cost, bytes_accessed=cost, transcendentals=0),
        name=name,
    )


def per_device(
    prognostic, metric, first_flux, second_flux, neighbour_face, orientation, coupling, damping
):
    fields, levels = prognostic.shape[:2]
    lanes = prognostic.shape[-1]
    state = prognostic.reshape(fields * levels * POINTS, lanes)
    metric = metric.reshape(POINTS, lanes)
    neighbour_face = neighbour_face.reshape(4, lanes)
    orientation = orientation.reshape(4, lanes)
    coupling = coupling.reshape(4, coupling.shape[1], NODES, lanes)
    damping = damping.reshape(NODES, lanes)
    tables, _ = operator_tables(lanes)

    def shifts(axis):
        size = lax.axis_size(axis)
        up = [(i, (i + 1) % size) for i in range(size)]
        return up, [(j, i) for i, j in up]

    def exchange(arrays):
        size = lax.axis_size("vz")
        moved = [arrays[0]]
        for way in range(1, size):
            moved.append(lax.ppermute(arrays[way], "vz", [(i, i ^ way) for i in range(size)]))
        return moved

    first_up, first_down = shifts("hy")
    second_up, second_down = shifts("hx")
    east_table = jnp.stack([neighbour_face[1], orientation[1]])
    west_table = jnp.stack([neighbour_face[0], orientation[0]])
    table_west = lax.ppermute(east_table, "hy", first_up)
    table_east = lax.ppermute(west_table, "hy", first_down)

    rows = fields * levels
    edge = (rows, lanes)
    to_up, to_down = call(edge_kernel, [edge, edge], [VMEM], cost=1000, name="edge")(state)
    from_down = lax.ppermute(to_up, "hx", second_up)
    from_up = lax.ppermute(to_down, "hx", second_down)

    face = (rows * NODES, lanes)
    to_west, to_east = call(face_kernel, [face, face], [VMEM] * 3, cost=1000, name="face")(
        state, table_west, table_east
    )
    from_east = lax.ppermute(to_west, "hy", first_down)
    from_west = lax.ppermute(to_east, "hy", first_up)

    (part,) = call(
        element_kernel,
        [state.shape],
        [VMEM] * 6 + [SMEM] * 2 + [VMEM],
        [
            pltpu.VMEM((levels * 8 * fields, lanes), jnp.float32),
            pltpu.VMEM((fields * POINTS, lanes), jnp.bfloat16),
            pltpu.VMEM((fields * POINTS, lanes), jnp.bfloat16),
        ],
        cost=4000000,
        name="element",
    )(
        state,
        from_down,
        from_up,
        neighbour_face,
        orientation,
        metric,
        first_flux,
        second_flux,
        jnp.asarray(tables),
    )
    column = (coupling.shape[1], NODES, lanes)
    factors = call(factor_kernel, [column] * 5, [VMEM] * 2, cost=4000000, name="factor")(
        coupling, damping
    )

    nodes = (0, 1, 2, 3)
    count = len(nodes)
    block = ((levels + 2) * count, lanes)
    theta, *sends = call(
        functools.partial(pack_kernel, nodes),
        [(levels * POINTS, lanes)] + [block] * NODES,
        [VMEM] * 4 + [SMEM],
        [
            pltpu.VMEM((NODES,) + block, jnp.float32),
            pltpu.VMEM((NODES * count, levels + 2 * ROWS + 4, lanes), jnp.float32),
        ],
        cost=1000,
        name="pack",
    )(part, from_west, from_east, metric, first_flux)
    cube = (levels + 2, count, lanes)
    received = [x.reshape(cube) for x in exchange(sends)]
    (done,) = call(
        finish_section_kernel,
        [(3 * levels * POINTS, lanes)],
        [VMEM] * 4 + [SMEM],
        cost=4000000,
        name="finish",
    )(part, from_west, from_east, metric, first_flux)
    speeds = call(
        solve_kernel,
        [cube] * NODES,
        [VMEM] * (5 + NODES),
        [
            pltpu.VMEM(column, jnp.float32),
            pltpu.VMEM((NODES, 2, count, lanes), jnp.float32),
            pltpu.VMEM((column[0] + 2,) + column[1:], jnp.float32),
        ],
        cost=1000,
        name="solve",
    )(*factors, *received)
    returned = exchange([x.reshape(block) for x in speeds])
    updated = pl.pallas_call(
        functools.partial(update_kernel, nodes),
        out_shape=jax.ShapeDtypeStruct(state.shape, jnp.float32),
        in_specs=[VMEM] * (2 + NODES),
        out_specs=VMEM,
        scratch_shapes=[pltpu.VMEM((NODES,) + block, jnp.float32)],
        compiler_params=pltpu.CompilerParams(vmem_limit_bytes=24 * 1024 * 1024),
        name="update",
    )(done, theta, *returned)
    return updated.reshape(prognostic.shape)


def solution(mesh):
    placed = (
        P(None, "vz", None, None, "hy", "hx"),
        P(None, None, "hy", "hx"),
        P(),
        P(),
        P(None, "hy", "hx"),
        P(None, "hy", "hx"),
        P(None, None, "vz", None, "hy", "hx"),
        P("vz", None, "hy", "hx"),
    )
    return jax.shard_map(
        per_device,
        mesh=mesh,
        in_specs=placed,
        out_specs=P(None, "vz", None, None, "hy", "hx"),
        check_vma=False,
    )
```

time: 134 us -> 36.5 us (0.27); the launches traced: 132 us -> 36.3 us
  other arithmetic: 42.9 us -> 0.02 us
  waiting for transfers between devices: 28 us -> 11.7 us
  local copies, waits for them, and re-layouts: 18.3 us -> 2.35 us
  blocking collectives: 13 us -> 0 us
  matrix products: 9.9 us -> 0 us
  between operations: 7.52 us -> 0.17 us
  Pallas kernels: 0 us -> 6.25 us
  starting transfers between devices: 12.7 us -> 15.9 us
    sub x41 -> x0, other arithmetic: 14 us -> none  [the longest x34 10.4 us: solve_unrolled(): scaled[height] - ratios[height] * next_one - seconds[height] * next_two]
    div x23 -> x0, other arithmetic: 13.4 us -> none  [the longest x21 12.6 us: solve_unrolled(): (source[height] - entry_a[height] * far_value - reduced * near_value) / p...]
    all_to_all x1 -> x0, blocking collectives: 13 us -> none  [per_device(): lax.all_to_all(jnp.stack([vertical_speed, speed_jump]), 'vz', split_axis=...]
    all_to_all x1 -> x0, waiting for transfers between devices: 10.8 us -> none  [per_device(): lax.all_to_all(section_state[3:5], 'vz', split_axis=2, concat_axis=1, til...]
    dot_general x6 -> x0, matrix products: 9.9 us -> none  [the longest x1 2.86 us: section_values(): jnp.einsum('cj,fljiab->flciab', derivative, flux_second, precision=highest)]
    ppermute x8 -> x12, starting transfers between devices: 7.82 us -> 15.9 us  [the longest x6 8.9 us: exchange(): lax.ppermute(arrays[way], 'vz', [(i, i ^ way) for i in range(size)])]
    pallas_call x0 -> x8, Pallas kernels: none -> 6.25 us  [the longest x1 1.66 us: per_device(): call(element_kernel, [state.shape], [VMEM] * 6 + [SMEM] * 2 + [VMEM], [pl...]
    ppermute x8 -> x12, waiting for transfers between devices: 17.2 us -> 11.7 us  [the longest x6 6.61 us: exchange(): lax.ppermute(arrays[way], 'vz', [(i, i ^ way) for i in range(size)])]
  transfers between devices with their start and end apart: 9 -> 12, of which waited for: 5 -> 7; matrix products, arithmetic and copies ran while one was open for 24% -> 0% of each run, Pallas kernels for 0% -> 10%
where the time goes in v1:
time: 36.5 us; the launch traced here: 36.3 us
  starting transfers between devices  15.9 us (44%)
  waiting for transfers between devices  11.7 us (32%)
  Pallas kernels  6.25 us (17%)
  local copies, waits for them, and re-layouts  2.35 us (6%)
    ppermute x6, starting transfers between devices, exchange(): lax.ppermute(arrays[way], 'vz', [(i, i ^ way) for i in range(size)])  8.9 us
    ppermute x6, waiting for transfers between devices, exchange(): lax.ppermute(arrays[way], 'vz', [(i, i ^ way) for i in range(size)])  6.61 us
    ppermute x1, starting transfers between devices, per_device(): from_west = lax.ppermute(to_east, 'hy', first_up)  2.35 us
    ppermute x1, waiting for transfers between devices, per_device(): from_down = lax.ppermute(to_up, 'hx', second_up)  2.19 us
    ppermute x1, starting transfers between devices, per_device(): table_east = lax.ppermute(west_table, 'hy', first_down)  2.03 us
    ppermute x1, starting transfers between devices, per_device(): from_down = lax.ppermute(to_up, 'hx', second_up)  1.72 us
    pallas_call x1, Pallas kernels, per_device(): call(element_kernel, [state.shape], [VMEM] * 6 + [SMEM] * 2 + [VMEM], [pl...  1.66 us
    unnamed x18, local copies, waits for them, and re-layouts  1.64 us
  transfers between devices with their start and end apart: 12, of which 7 were waited for; matrix products, arithmetic and copies ran while one was open for 0% of the time, Pallas kernels for 10%

profile of v1, /device:TPU:0, one launch (start us, length us, event | category | flops | bytes accessed | tf_op | source)
XLA Modules:
  0.0 36.3 jit_solution(9214245923701343858)
XLA Ops:
  0.0 0.7 %slice_bitcast_fusion = (s32[1,128]{1,0:T(1,128)S(1)}, s32[1,128]{1,0:T(1,128)S(1)}, s32[1,128]{1,0:T(1,128)S(1)}, s32[1,128]{1,0:T(1,128)S(1)}) fusion(s32[4,1,128]{2,1,0:T(1,128)} %param.14, s32[4,1,128]{2,1,0:T(1,128)} %param.13), kind=kLoop, calls=%fused_computation.2 | loop fusion | bytes 4096 | tf_op jit(solution)/shard_map/slice | solution.py:424
  0.7 0.5 %collective-permute-start.2 = (s32[2,128]{1,0:T(2,128)S(1)}, s32[2,128]{1,0:T(2,128)S(1)}, u32[]{:S(2)}, u32[]{:S(2)}) collective-permute-start(s32[2,128]{1,0:T(2,128)S(1)} %pad_add_fusion), channel_id=1, source_target_pairs={{0,4},{4,8},{8,12},{12,0},{1,5},{5,9},{9,13},{13,1},{2,6},{6,10},{... | collective-permute-start | bytes 3080 | tf_op jit(solution)/shard_map/ppermute | solution.py:425
  1.2 2.0 %collective-permute-start.3 = (s32[2,128]{1,0:T(2,128)S(1)}, s32[2,128]{1,0:T(2,128)S(1)}, u32[]{:S(2)}, u32[]{:S(2)}) collective-permute-start(s32[2,128]{1,0:T(2,128)S(1)} %pad_add_fusion.1), channel_id=1, source_target_pairs={{4,0},{8,4},{12,8},{0,12},{5,1},{9,5},{13,9},{1,13},{6,2},{10,6},{... | collective-permute-start | bytes 3080 | tf_op jit(solution)/shard_map/ppermute | solution.py:426
  3.3 1.2 %collective-permute-done.2.table_west = s32[2,128]{1,0:T(2,128)S(1)} collective-permute-done((s32[2,128]{1,0:T(2,128)S(1)}, s32[2,128]{1,0:T(2,128)S(1)}, u32[]{:S(2)}, u32[]{:S(2)}) %collective-permute-start.2) | collective-permute-done | bytes 1056 | tf_op jit(solution)/shard_map/ppermute | solution.py:425
  4.4 0.1 collective-permute-done.3.table_east
  4.6 0.0 copy-start
  4.6 1.1 %copy-done = f32[5,20,4,4,1,128]{5,4,3,2,1,0:T(1,128)S(1)} copy-done((f32[5,20,4,4,1,128]{5,4,3,2,1,0:T(1,128)S(1)}, f32[5,20,4,4,1,128]{5,4,3,2,1,0:T(1,128)}, u32[]{:S(2)}) %copy-start) | copy-done | bytes 819224
  5.7 0.2 face.1
  5.9 2.4 %collective-permute-start.4 = (f32[400,128]{1,0:T(8,128)S(1)}, f32[400,128]{1,0:T(8,128)S(1)}, u32[]{:S(2)}, u32[]{:S(2)}) collective-permute-start(f32[400,128]{1,0:T(8,128)S(1)} %get-tuple-element.25), channel_id=1, source_target_pairs={{0,4},{4,8},{8,12},{12,0},{1,5},{5,9},{9,13},{13,1},{2,6},{6,10},{... | collective-permute-start | bytes 614408 | tf_op jit(solution)/shard_map/ppermute | solution.py:439
  8.3 0.0 copy-start.3
  8.3 0.0 collective-permute-start.5
  8.3 0.0 copy-start.6
  8.3 0.0 copy-start.7
  8.3 0.2 edge.1
  8.5 0.0 copy-start.2
  8.5 1.7 %collective-permute-start = (f32[100,128]{1,0:T(8,128)S(1)}, f32[100,128]{1,0:T(8,128)S(1)}, u32[]{:S(2)}, u32[]{:S(2)}) collective-permute-start(f32[100,128]{1,0:T(8,128)S(1)} %get-tuple-element.23), channel_id=1, source_target_pairs={{0,16},{16,0},{1,17},{17,1},{2,18},{18,2},{3,19},{19,3},{4,20},{20... | collective-permute-start | bytes 153608 | tf_op jit(solution)/shard_map/ppermute | solution.py:431
  10.3 0.4 %collective-permute-start.1 = (f32[100,128]{1,0:T(8,128)S(1)}, f32[100,128]{1,0:T(8,128)S(1)}, u32[]{:S(2)}, u32[]{:S(2)}) collective-permute-start(f32[100,128]{1,0:T(8,128)S(1)} %get-tuple-element.24), channel_id=1, source_target_pairs={{16,0},{0,16},{17,1},{1,17},{18,2},{2,18},{19,3},{3,19},{20,4},{4,... | collective-permute-start | bytes 153608 | tf_op jit(solution)/shard_map/ppermute | solution.py:432
  10.6 2.2 %collective-permute-done.from_down = f32[100,128]{1,0:T(8,128)S(1)} collective-permute-done((f32[100,128]{1,0:T(8,128)S(1)}, f32[100,128]{1,0:T(8,128)S(1)}, u32[]{:S(2)}, u32[]{:S(2)}) %collective-permute-start) | collective-permute-done | bytes 51232 | tf_op jit(solution)/shard_map/ppermute | solution.py:431
  12.8 1.6 %collective-permute-done.1.from_up = f32[100,128]{1,0:T(8,128)S(1)} collective-permute-done((f32[100,128]{1,0:T(8,128)S(1)}, f32[100,128]{1,0:T(8,128)S(1)}, u32[]{:S(2)}, u32[]{:S(2)}) %collective-permute-start.1) | collective-permute-done | bytes 51232 | tf_op jit(solution)/shard_map/ppermute | solution.py:432
  14.4 0.0 copy-done.3
  14.4 0.0 copy-done.4
  14.4 0.0 copy-done.5
  14.4 0.0 copy-done.6
  14.4 0.0 copy-done.7
  14.4 0.0 copy-done.2
  14.4 1.7 %element.1.part = f32[1600,128]{1,0:T(8,128)S(1)} custom-call(f32[1600,128]{1,0:T(8,128)S(1)} %bitcast.27, f32[100,128]{1,0:T(8,128)S(1)} %collective-permute-done.from_down, f32[100,128]{1,0:T(8,128)S(1)} %collective-permute-done.1.from_up, s32[4,128]{1,0:T(4,128)S(1)} %bitcast.37, s32[4,128]{1,0:T(4,128)S(1)} %bitcast.38, f32[16,128]{1,0:T(8,128)S(1)} %bitcast.29, ...), custom_call_target="tpu_custom_call" | custom-call | flops 4000000 | bytes 4000000 | tf_op jit(solution)/shard_map/element/pallas_call | solution.py:441
  16.1 0.0 copy-start.1
  16.1 0.0 collective-permute-done.4.from_west
  16.1 0.0 collective-permute-done.5.from_east
  16.1 0.9 %pack.1 = (f32[320,128]{1,0:T(8,128)S(1)}, f32[88,128]{1,0:T(8,128)S(1)}, f32[88,128]{1,0:T(8,128)S(1)}, f32[88,128]{1,0:T(8,128)S(1)}, f32[88,128]{1,0:T(8,128)S(1)}) custom-call(f32[1600,128]{1,0:T(8,128)S(1)} %element.1.part, f32[400,128]{1,0:T(8,128)S(1)} %collective-permute-done.4.from_west, f32[400,128]{1,0:T(8,128)S(1)} %collective-permute-done.5.from_east, ...), custom_call_target="tpu_custom_call" | custom-call | flops 1000 | bytes 1000 | tf_op jit(solution)/shard_map/pack/pallas_call | solution.py:471
  17.0 1.6 %collective-permute-start.6 = (f32[88,128]{1,0:T(8,128)S(1)}, f32[88,128]{1,0:T(8,128)S(1)}, u32[]{:S(2)}, u32[]{:S(2)}) collective-permute-start(f32[88,128]{1,0:T(8,128)S(1)} %get-tuple-element.34), channel_id=1, source_target_pairs={{0,1},{1,0},{2,3},{3,2},{4,5},{5,4},{6,7},{7,6},{8,9},{9,8},{10,11... | collective-permute-start | bytes 135176 | tf_op jit(solution)/shard_map/ppermute | solution.py:418
  18.7 2.6 %collective-permute-start.7 = (f32[88,128]{1,0:T(8,128)S(1)}, f32[88,128]{1,0:T(8,128)S(1)}, u32[]{:S(2)}, u32[]{:S(2)}) collective-permute-start(f32[88,128]{1,0:T(8,128)S(1)} %get-tuple-element.35), channel_id=1, source_target_pairs={{0,2},{1,3},{2,0},{3,1},{4,6},{5,7},{6,4},{7,5},{8,10},{9,11},{10,... | collective-permute-start | bytes 135176 | tf_op jit(solution)/shard_map/ppermute | solution.py:418
  21.3 0.2 collective-permute-start.8
  21.5 0.0 copy-done.1
  21.5 0.5 %copy-done.8 = f32[1,4,1,128]{3,2,1,0:T(1,128)S(1)} copy-done((f32[1,4,1,128]{3,2,1,0:T(1,128)S(1)}, f32[1,4,1,128]{3,2,1,0:T(1,128)}, u32[]{:S(2)}) %copy-start.8) | copy-done | bytes 2072
  22.0 0.7 %factor.1 = (f32[80,4,128]{2,1,0:T(4,128)S(1)}, f32[80,4,128]{2,1,0:T(4,128)S(1)}, f32[80,4,128]{2,1,0:T(4,128)S(1)}, f32[80,4,128]{2,1,0:T(4,128)S(1)}, f32[80,4,128]{2,1,0:T(4,128)S(1)}) custom-call(f32[4,80,4,128]{3,2,1,0:T(4,128)S(1)} %bitcast.28, f32[4,128]{1,0:T(4,128)S(1)} %bitcast.39), custom_call_target="tpu_custom_call" | custom-call | flops 4000000 | bytes 4000000 | tf_op jit(solution)/shard_map/factor/pallas_call | solution.py:464
  22.7 0.0 collective-permute-done.6
  22.7 1.9 %collective-permute-done.7 = f32[88,128]{1,0:T(8,128)S(1)} collective-permute-done((f32[88,128]{1,0:T(8,128)S(1)}, f32[88,128]{1,0:T(8,128)S(1)}, u32[]{:S(2)}, u32[]{:S(2)}) %collective-permute-start.7) | collective-permute-done | bytes 45088 | tf_op jit(solution)/shard_map/ppermute | solution.py:418
  24.6 3.1 %collective-permute-done.8 = f32[88,128]{1,0:T(8,128)S(1)} collective-permute-done((f32[88,128]{1,0:T(8,128)S(1)}, f32[88,128]{1,0:T(8,128)S(1)}, u32[]{:S(2)}, u32[]{:S(2)}) %collective-permute-start.8) | collective-permute-done | bytes 45088 | tf_op jit(solution)/shard_map/ppermute | solution.py:418
  27.7 0.4 %solve.1 = (f32[22,4,128]{2,1,0:T(4,128)S(1)}, f32[22,4,128]{2,1,0:T(4,128)S(1)}, f32[22,4,128]{2,1,0:T(4,128)S(1)}, f32[22,4,128]{2,1,0:T(4,128)S(1)}) custom-call(f32[80,4,128]{2,1,0:T(4,128)S(1)} %get-tuple-element.28.far, f32[80,4,128]{2,1,0:T(4,128)S(1)} %get-tuple-element.29.near, f32[80,4,128]{2,1,0:T(4,128)S(1)} %get-tuple-element.30.inverse, ...), custom_call_target="tpu_custom_call" | custom-call | flops 1000 | bytes 1000 | tf_op jit(solution)/shard_map/solve/pallas_call | solution.py:491
  28.1 0.1 collective-permute-start.9
  28.2 0.5 %collective-permute-start.10 = (f32[88,128]{1,0:T(8,128)S(1)}, f32[88,128]{1,0:T(8,128)S(1)}, u32[]{:S(2)}, u32[]{:S(2)}) collective-permute-start(f32[88,128]{1,0:T(8,128)S(1)} %bitcast.41), channel_id=1, source_target_pairs={{0,2},{1,3},{2,0},{3,1},{4,6},{5,7},{6,4},{7,5},{8,10},{9,11},{10,... | collective-permute-start | bytes 135176 | tf_op jit(solution)/shard_map/ppermute | solution.py:418
  28.6 3.9 %collective-permute-start.11 = (f32[88,128]{1,0:T(8,128)S(1)}, f32[88,128]{1,0:T(8,128)S(1)}, u32[]{:S(2)}, u32[]{:S(2)}) collective-permute-start(f32[88,128]{1,0:T(8,128)S(1)} %bitcast.40), channel_id=1, source_target_pairs={{0,3},{1,2},{2,1},{3,0},{4,7},{5,6},{6,5},{7,4},{8,11},{9,10},{10,... | collective-permute-start | bytes 135176 | tf_op jit(solution)/shard_map/ppermute | solution.py:418
  32.6 0.9 %finish.1.done = f32[960,128]{1,0:T(8,128)S(1)} custom-call(f32[1600,128]{1,0:T(8,128)S(1)} %element.1.part, f32[400,128]{1,0:T(8,128)S(1)} %collective-permute-done.4.from_west, f32[400,128]{1,0:T(8,128)S(1)} %collective-permute-done.5.from_east, f32[16,128]{1,0:T(8,128)S(1)} %bitcast.31, f32[5,5]{1,0:T(8,128)S(1)} %copy-done.4), custom_call_target="tpu_custom_call" | custom-call | flops 4000000 | bytes 4000000 | tf_op jit(solution)/shard_map/finish/pallas_call | solution.py:484
  33.4 0.0 collective-permute-done.9.rest_1_
  33.5 0.0 collective-permute-done.10.rest_2_
  33.5 1.6 %collective-permute-done.11.rest_3_ = f32[88,128]{1,0:T(8,128)S(1)} collective-permute-done((f32[88,128]{1,0:T(8,128)S(1)}, f32[88,128]{1,0:T(8,128)S(1)}, u32[]{:S(2)}, u32[]{:S(2)}) %collective-permute-start.11) | collective-permute-done | bytes 45088 | tf_op jit(solution)/shard_map/ppermute | solution.py:418
  35.1 1.3 %update.1 = f32[1600,128]{1,0:T(8,128)} custom-call(f32[960,128]{1,0:T(8,128)S(1)} %finish.1.done, f32[320,128]{1,0:T(8,128)S(1)} %get-tuple-element.27.theta, f32[88,128]{1,0:T(8,128)S(1)} %bitcast.32, f32[88,128]{1,0:T(8,128)S(1)} %collective-permute-done.9.rest_1_, f32[88,128]{1,0:T(8,128)S(1)} %collective-permute-done.10.rest_2_, ...), custom_call_target="tpu_custom_call" | custom-call | tf_op jit(solution)/shard_map/update/pallas_call | solution.py:504
  (5 shorter events, 0.0 us)
Async XLA Ops:
  0.7 3.7 %collective-permute-start.2 = (s32[2,128]{1,0:T(2,128)S(1)}, s32[2,128]{1,0:T(2,128)S(1)}, u32[]{:S(2)}, u32[]{:S(2)}) collective-permute-start(s32[2,128]{1,0:T(2,128)S(1)} %pad_add_fusion), channel_id=1, source_target_pairs={{0,4},{4,8},{8,12},{12,0},{1,5},{5,9},{9,13},{13,1},{2,6},{6,10},{... | collective-permute-start | bytes 3080 | tf_op jit(solution)/shard_map/ppermute | solution.py:425
  1.2 3.3 %collective-permute-start.3 = (s32[2,128]{1,0:T(2,128)S(1)}, s32[2,128]{1,0:T(2,128)S(1)}, u32[]{:S(2)}, u32[]{:S(2)}) collective-permute-start(s32[2,128]{1,0:T(2,128)S(1)} %pad_add_fusion.1), channel_id=1, source_target_pairs={{4,0},{8,4},{12,8},{0,12},{5,1},{9,5},{13,9},{1,13},{6,2},{10,6},{... | collective-permute-start | bytes 3080 | tf_op jit(solution)/shard_map/ppermute | solution.py:426
  4.6 1.1 %copy-start = (f32[5,20,4,4,1,128]{5,4,3,2,1,0:T(1,128)S(1)}, f32[5,20,4,4,1,128]{5,4,3,2,1,0:T(1,128)}, u32[]{:S(2)}) copy-start(f32[5,20,4,4,1,128]{5,4,3,2,1,0:T(1,128)} %param.9) | copy-start | bytes 2457604
  5.9 10.2 %collective-permute-start.4 = (f32[400,128]{1,0:T(8,128)S(1)}, f32[400,128]{1,0:T(8,128)S(1)}, u32[]{:S(2)}, u32[]{:S(2)}) collective-permute-start(f32[400,128]{1,0:T(8,128)S(1)} %get-tuple-element.25), channel_id=1, source_target_pairs={{0,4},{4,8},{8,12},{12,0},{1,5},{5,9},{9,13},{13,1},{2,6},{6,10},{... | collective-permute-start | bytes 614408 | tf_op jit(solution)/shard_map/ppermute | solution.py:439
  8.3 6.2 %copy-start.3 = (f32[112,128]{1,0:T(8,128)S(1)}, f32[112,128]{1,0:T(8,128)}, u32[]{:S(2)}) copy-start(f32[112,128]{1,0:T(8,128)} %constant.2.clone.tables) | copy-start | bytes 172036
  8.3 7.9 %collective-permute-start.5 = (f32[400,128]{1,0:T(8,128)S(1)}, f32[400,128]{1,0:T(8,128)S(1)}, u32[]{:S(2)}, u32[]{:S(2)}) collective-permute-start(f32[400,128]{1,0:T(8,128)S(1)} %get-tuple-element.26), channel_id=1, source_target_pairs={{4,0},{8,4},{12,8},{0,12},{5,1},{9,5},{13,9},{1,13},{6,2},{10,6},{... | collective-permute-start | bytes 614408 | tf_op jit(solution)/shard_map/ppermute | solution.py:438
  8.3 6.2 %copy-start.4 = (f32[5,5]{1,0:T(8,128)S(1)}, f32[5,5]{1,0:T(8,128)}, u32[]{:S(2)}) copy-start(f32[5,5]{1,0:T(8,128)} %flux.3) | copy-start | bytes 304
  8.3 6.2 %copy-start.5 = (s32[4,1,128]{2,1,0:T(1,128)S(1)}, s32[4,1,128]{2,1,0:T(1,128)}, u32[]{:S(2)}) copy-start(s32[4,1,128]{2,1,0:T(1,128)} %param.13) | copy-start | bytes 6148
  8.3 6.1 %copy-start.6 = (s32[4,1,128]{2,1,0:T(1,128)S(1)}, s32[4,1,128]{2,1,0:T(1,128)}, u32[]{:S(2)}) copy-start(s32[4,1,128]{2,1,0:T(1,128)} %param.14) | copy-start | bytes 6148
  8.3 6.1 %copy-start.7 = (f32[5,5]{1,0:T(8,128)S(1)}, f32[5,5]{1,0:T(8,128)}, u32[]{:S(2)}) copy-start(f32[5,5]{1,0:T(8,128)} %second_flux.1) | copy-start | bytes 304
  8.5 5.9 %copy-start.2 = (f32[4,4,1,128]{3,2,1,0:T(1,128)S(1)}, f32[4,4,1,128]{3,2,1,0:T(1,128)}, u32[]{:S(2)}) copy-start(f32[4,4,1,128]{3,2,1,0:T(1,128)} %param.10) | copy-start | bytes 24580
  8.5 4.3 %collective-permute-start = (f32[100,128]{1,0:T(8,128)S(1)}, f32[100,128]{1,0:T(8,128)S(1)}, u32[]{:S(2)}, u32[]{:S(2)}) collective-permute-start(f32[100,128]{1,0:T(8,128)S(1)} %get-tuple-element.23), channel_id=1, source_target_pairs={{0,16},{16,0},{1,17},{17,1},{2,18},{18,2},{3,19},{19,3},{4,20},{20... | collective-permute-start | bytes 153608 | tf_op jit(solution)/shard_map/ppermute | solution.py:431
  10.3 4.1 %collective-permute-start.1 = (f32[100,128]{1,0:T(8,128)S(1)}, f32[100,128]{1,0:T(8,128)S(1)}, u32[]{:S(2)}, u32[]{:S(2)}) collective-permute-start(f32[100,128]{1,0:T(8,128)S(1)} %get-tuple-element.24), channel_id=1, source_target_pairs={{16,0},{0,16},{17,1},{1,17},{18,2},{2,18},{19,3},{3,19},{20,4},{4,... | collective-permute-start | bytes 153608 | tf_op jit(solution)/shard_map/ppermute | solution.py:432
  16.1 5.4 %copy-start.1 = (f32[4,80,1,4,1,128]{5,4,3,2,1,0:T(1,128)S(1)}, f32[4,80,1,4,1,128]{5,4,3,2,1,0:T(1,128)}, u32[]{:S(2)}) copy-start(f32[4,80,1,4,1,128]{5,4,3,2,1,0:T(1,128)} %param.15) | copy-start | bytes 1966084
  17.0 5.6 %collective-permute-start.6 = (f32[88,128]{1,0:T(8,128)S(1)}, f32[88,128]{1,0:T(8,128)S(1)}, u32[]{:S(2)}, u32[]{:S(2)}) collective-permute-start(f32[88,128]{1,0:T(8,128)S(1)} %get-tuple-element.34), channel_id=1, source_target_pairs={{0,1},{1,0},{2,3},{3,2},{4,5},{5,4},{6,7},{7,6},{8,9},{9,8},{10,11... | collective-permute-start | bytes 135176 | tf_op jit(solution)/shard_map/ppermute | solution.py:418
  18.7 5.9 %collective-permute-start.7 = (f32[88,128]{1,0:T(8,128)S(1)}, f32[88,128]{1,0:T(8,128)S(1)}, u32[]{:S(2)}, u32[]{:S(2)}) collective-permute-start(f32[88,128]{1,0:T(8,128)S(1)} %get-tuple-element.35), channel_id=1, source_target_pairs={{0,2},{1,3},{2,0},{3,1},{4,6},{5,7},{6,4},{7,5},{8,10},{9,11},{10,... | collective-permute-start | bytes 135176 | tf_op jit(solution)/shard_map/ppermute | solution.py:418
  21.3 0.7 %copy-start.8 = (f32[1,4,1,128]{3,2,1,0:T(1,128)S(1)}, f32[1,4,1,128]{3,2,1,0:T(1,128)}, u32[]{:S(2)}) copy-start(f32[1,4,1,128]{3,2,1,0:T(1,128)} %param.16) | copy-start | bytes 6148
  21.3 6.4 %collective-permute-start.8 = (f32[88,128]{1,0:T(8,128)S(1)}, f32[88,128]{1,0:T(8,128)S(1)}, u32[]{:S(2)}, u32[]{:S(2)}) collective-permute-start(f32[88,128]{1,0:T(8,128)S(1)} %get-tuple-element.36), channel_id=1, source_target_pairs={{0,3},{1,2},{2,1},{3,0},{4,7},{5,6},{6,5},{7,4},{8,11},{9,10},{10,... | collective-permute-start | bytes 135176 | tf_op jit(solution)/shard_map/ppermute | solution.py:418
  28.1 5.3 %collective-permute-start.9 = (f32[88,128]{1,0:T(8,128)S(1)}, f32[88,128]{1,0:T(8,128)S(1)}, u32[]{:S(2)}, u32[]{:S(2)}) collective-permute-start(f32[88,128]{1,0:T(8,128)S(1)} %bitcast.42), channel_id=1, source_target_pairs={{0,1},{1,0},{2,3},{3,2},{4,5},{5,4},{6,7},{7,6},{8,9},{9,8},{10,11... | collective-permute-start | bytes 135176 | tf_op jit(solution)/shard_map/ppermute | solution.py:418
  28.2 5.3 %collective-permute-start.10 = (f32[88,128]{1,0:T(8,128)S(1)}, f32[88,128]{1,0:T(8,128)S(1)}, u32[]{:S(2)}, u32[]{:S(2)}) collective-permute-start(f32[88,128]{1,0:T(8,128)S(1)} %bitcast.41), channel_id=1, source_target_pairs={{0,2},{1,3},{2,0},{3,1},{4,6},{5,7},{6,4},{7,5},{8,10},{9,11},{10,... | collective-permute-start | bytes 135176 | tf_op jit(solution)/shard_map/ppermute | solution.py:418
  28.6 6.4 %collective-permute-start.11 = (f32[88,128]{1,0:T(8,128)S(1)}, f32[88,128]{1,0:T(8,128)S(1)}, u32[]{:S(2)}, u32[]{:S(2)}) collective-permute-start(f32[88,128]{1,0:T(8,128)S(1)} %bitcast.40), channel_id=1, source_target_pairs={{0,3},{1,2},{2,1},{3,0},{4,7},{5,6},{6,5},{7,4},{8,11},{9,10},{10,... | collective-permute-start | bytes 135176 | tf_op jit(solution)/shard_map/ppermute | solution.py:418
